TPU v7x, 256 devices: a whole 4x4x8 slice. The times are simulated.
256 devices in a mesh: gy: 16 (over y, x), gz: 16 (over z, core).
Axes of the slice: x: 4, y: 4, z: 8, core: 2. Of those that a mesh axis runs over, the one named last changes fastest.
Arguments:
- right_side: float32 [256, 256, 512], P('gz', 'gy'), may hold values from -6 to 6
- cotangent: float32 [256, 256, 512], P('gz', 'gy'), may hold values from -6 to 6
- phase: int32 [256, 256, 512], P('gz', 'gy'), may hold values 0 or 1
Outputs:
- correction: float32 [256, 256, 512], P('gz', 'gy')
- transposed: float32 [256, 256, 512], P('gz', 'gy')
All inputs are finite; a program needn't handle non-finite values. No bound on the sum of `phase` on one device may be relied on, other than what follows from the above.
Results may differ from a plain program's by a relative error of at most 0.0001.
Values sent between devices are 32-bit elements; how exact they have to be, the bound alone decides.
A program may use at most 192 MiB of HBM per device.

v0:
```python
import functools

import jax
import jax.numpy as jnp
from jax import lax
from jax.experimental import pallas as pl
from jax.experimental.pallas import tpu as pltpu
from jax.sharding import PartitionSpec as P

MESH = pl.DeviceIdType.MESH
RING = 16
MID = 1.125
HALF = 0.875
RATIO = MID / HALF
FIRST = 1.0 / RATIO
SECOND = 1.0 / (2.0 * RATIO - FIRST)
C1 = SECOND * FIRST
C2 = 2.0 * SECOND / HALF
LIGHT = 1.0
HEAVY = 1.0 / 8.0
AROUND = tuple((a, b) for a in (-1, 0, 1) for b in (-1, 0, 1) if (a, b) != (0, 0))
F32 = jnp.float32


def flat(values):
    return values.reshape((-1,) + values.shape[-2:])


def sub_iota(shape):
    return lax.broadcasted_iota(jnp.int32, shape, len(shape) - 2)


def lane_iota(shape):
    return lax.broadcasted_iota(jnp.int32, shape, len(shape) - 1)


def sub_take(values, index_of):
    rows = flat(values)
    if rows.shape[0] == 1:
        rows = rows[0]
    index = index_of(sub_iota(rows.shape))
    return jnp.take_along_axis(rows, index, axis=rows.ndim - 2).reshape(values.shape)


def lane_take(values, index_of):
    rows = flat(values)
    if rows.shape[0] == 1:
        rows = rows[0]
    index = index_of(sub_iota(rows.shape), lane_iota(rows.shape))
    return jnp.take_along_axis(rows, index, axis=rows.ndim - 1).reshape(values.shape)


def sub_roll(values, shift):
    rows = flat(values)
    return pltpu.roll(rows, shift % 8, 1).reshape(values.shape)


def lane_roll(values, shift):
    rows = flat(values)
    return pltpu.roll(rows, shift % 128, 2).reshape(values.shape)


class Level:
    def __init__(self, depth, refs):
        self.depth = depth
        self.scale = 0.5 * 0.25**depth
        self.mob, self.src, self.az, self.ay, self.ax, self.inv, self.val, self.smo, self.err, self.rem = refs

    def field_one(self, shape):
        if self.depth == 0:
            return sub_iota(shape) >= 4
        if self.depth == 1:
            return (sub_iota(shape) // 2) % 2 == 1
        if self.depth == 2:
            return sub_iota(shape) % 2 == 1
        return lane_iota(shape) >= 64

    def x_side(self, values, step):
        if self.depth <= 2:
            rolled = lane_roll(values, -step)
            if self.depth == 2:
                return rolled
            if self.depth == 0:
                other = sub_take(rolled, lambda s: (s // 4) * 4 + (s + step + 4) % 4)
            else:
                other = sub_take(rolled, lambda s: s + 1 - 2 * (s % 2))
            edge = 127 if step == 1 else 0
            return jnp.where(lane_iota(values.shape) == edge, other, rolled)
        wide = 2 ** (self.depth - 3)
        return lane_take(values, lambda s, l: (l // 64) * 64 + (l + step * wide + 64) % 64)

    def y_side(self, values, step):
        rows = {1: 4, 2: 2}.get(self.depth, 1)
        count = values.shape[1]
        if count == 1:
            other = values
        elif step == 1:
            other = jnp.concatenate([values[:, 1:], values[:, :1]], axis=1)
        else:
            other = jnp.concatenate([values[:, -1:], values[:, :-1]], axis=1)
        place = sub_iota(values.shape)
        edge = place < rows if step == 1 else place >= 8 - rows
        return sub_roll(jnp.where(edge, other, values), -step * rows)

    def coefficients(self, at, count, mask=None):
        here = self.mob[pl.ds(at, count)]
        up = self.scale * (here + self.mob[pl.ds(at + 1, count)])
        down = self.scale * (here + self.mob[pl.ds(at - 1, count)])
        right = self.scale * (here + self.y_side(here, 1))
        ahead = self.scale * (here + self.x_side(here, 1))
        diagonal = up + down + right + self.y_side(right, -1) + ahead + self.x_side(ahead, -1)
        self.az[pl.ds(at, count)] = up
        self.ay[pl.ds(at, count)] = right
        self.ax[pl.ds(at, count)] = ahead
        return self.masked_inverse(diagonal, mask)

    def masked_inverse(self, diagonal, mask):
        if mask is None:
            return 1.0 / diagonal
        return mask / (diagonal + (1.0 - mask))

    def operate(self, ref, at, count):
        here = ref[pl.ds(at, count)]
        total = self.az[pl.ds(at, count)] * (here - ref[pl.ds(at + 1, count)])
        total = total + self.az[pl.ds(at - 1, count)] * (here - ref[pl.ds(at - 1, count)])
        flux = self.ay[pl.ds(at, count)] * (here - self.y_side(here, 1))
        total = total + (flux - self.y_side(flux, -1))
        flux = self.ax[pl.ds(at, count)] * (here - self.x_side(here, 1))
        return here, total + (flux - self.x_side(flux, -1))

    def start(self, at, count):
        self.val[pl.ds(at, count)] = self.src[pl.ds(at, count)] * self.inv[pl.ds(at, count)] * (1.0 / MID)

    def smooth(self, at, count):
        here, applied = self.operate(self.val, at, count)
        rest = self.src[pl.ds(at, count)] - applied
        second = here + C1 * here + C2 * (self.inv[pl.ds(at, count)] * rest)
        self.smo[pl.ds(at, count)] = jnp.where(self.field_one(here.shape), here, second)

    def remainder(self, at, count):
        _, applied = self.operate(self.smo, at, count)
        return self.src[pl.ds(at, count)] - applied

    def correct(self, at, count):
        _, applied = self.operate(self.val, at, count)
        rest = self.src[pl.ds(at, count)] - applied
        self.rem[pl.ds(at, count)] = rest
        self.err[pl.ds(at, count)] = rest * self.inv[pl.ds(at, count)] * (1.0 / MID)

    def finish(self, at, count):
        here, applied = self.operate(self.err, at, count)
        rest = self.rem[pl.ds(at, count)] - applied
        second = C1 * here + C2 * (self.inv[pl.ds(at, count)] * rest)
        base = self.val[pl.ds(at, count)] + here
        return jnp.where(self.field_one(here.shape), base + second, base)


class Finest(Level):
    def coefficients(self, plane, low, count, mask):
        here = self.mob[plane + 1, pl.ds(low, count + 2)]
        mid = here[1:-1]
        up = self.scale * (mid + self.mob[plane + 2, pl.ds(low + 1, count)])
        down = self.scale * (mid + self.mob[plane, pl.ds(low + 1, count)])
        right = self.scale * (here[:-1] + here[1:])
        ahead = self.scale * (mid + self.x_side(mid, 1))
        diagonal = up + down + right[1:] + right[:-1] + ahead + self.x_side(ahead, -1)
        self.az[plane, pl.ds(low, count)] = up
        self.ay[plane, pl.ds(low, count)] = right[1:]
        self.ax[plane, pl.ds(low, count)] = ahead
        self.inv[plane, pl.ds(low, count)] = self.masked_inverse(diagonal, mask)

    def operate(self, ref, plane, low, count):
        wide = ref[plane, pl.ds(low - 1, count + 2)]
        here = wide[1:-1]
        part = pl.ds(low, count)
        total = self.az[plane, part] * (here - ref[plane + 1, part])
        total = total + self.az[plane - 1, part] * (here - ref[plane - 1, part])
        flux = self.ay[plane, pl.ds(low - 1, count + 1)] * (wide[:-1] - wide[1:])
        total = total + (flux[1:] - flux[:-1])
        flux = self.ax[plane, part] * (here - self.x_side(here, 1))
        return here, total + (flux - self.x_side(flux, -1))

    def start(self, plane, low, count):
        part = pl.ds(low, count)
        self.val[plane, part] = self.src[plane, part] * self.inv[plane, part] * (1.0 / MID)

    def smooth(self, plane, low, count):
        part = pl.ds(low, count)
        here, applied = self.operate(self.val, plane, low, count)
        rest = self.src[plane, part] - applied
        second = here + C1 * here + C2 * (self.inv[plane, part] * rest)
        self.smo[plane, part] = jnp.where(self.field_one(here.shape), here, second)

    def remainder(self, plane, low, count):
        _, applied = self.operate(self.smo, plane, low, count)
        return self.src[plane, pl.ds(low, count)] - applied

    def correct(self, plane, low, count):
        part = pl.ds(low, count)
        _, applied = self.operate(self.val, plane, low, count)
        rest = self.src[plane, part] - applied
        self.rem[plane, part] = rest
        self.err[plane, part] = rest * self.inv[plane, part] * (1.0 / MID)

    def finish(self, plane, low, count):
        part = pl.ds(low, count)
        here, applied = self.operate(self.err, plane, low, count)
        rest = self.rem[plane, part] - applied
        second = C1 * here + C2 * (self.inv[plane, part] * rest)
        base = self.val[plane, part] + here
        return jnp.where(self.field_one(here.shape), base + second, base)


def halves(values):
    return lane_take(values + lane_roll(values, -1), lambda s, l: (2 * l) % 128)


def restrict_0(planes):
    count = planes.shape[0] // 4
    four = planes.reshape((count, 4) + planes.shape[1:])
    out = []
    for pair in (0, 2):
        got = halves(four[:, pair] + four[:, pair + 1])
        left = sub_take(got, lambda s: ((s // 2) % 2) * 4 + 2 * (s % 2))
        right = sub_take(got, lambda s: ((s // 2) % 2) * 4 + 2 * (s % 2) + 1)
        out.append(jnp.where(lane_iota(got.shape) < 64, left, right))
    return 0.125 * jnp.where(sub_iota(out[0].shape) < 4, out[0], out[1])


def restrict_1(planes):
    got = halves(planes + sub_roll(planes, 4))
    left = sub_take(got, lambda s: (s % 2) * 2)
    right = sub_take(got, lambda s: (s % 2) * 2 + 1)
    both = jnp.where(lane_iota(got.shape) < 64, left, right)
    row = sub_iota(both[:, 0].shape) // 2
    out = jnp.where(row == 0, both[:, 0], both[:, 1])
    out = jnp.where(row == 2, both[:, 2], out)
    return 0.125 * jnp.where(row == 3, both[:, 3], out)


def restrict_2(planes):
    got = halves(planes + sub_roll(planes, -2))
    left = sub_take(got, lambda s: (4 * s) % 8)
    right = sub_take(got, lambda s: (4 * s + 1) % 8)
    return 0.125 * jnp.where(lane_iota(got.shape) < 64, left, right)


def restrict_whole(planes, depth):
    wide = 2 ** (depth - 3)
    got = planes + lane_take(planes, lambda s, l: l + wide - 2 * wide * ((l // wide) % 2))
    got = sub_take(got + sub_roll(got, -1), lambda s: (2 * s) % 8)
    count = got.shape[1]
    if count == 1:
        return 0.125 * got
    pairs = got.reshape((got.shape[0], count // 2, 2, 8, 128))
    low = sub_iota(pairs[:, :, 0].shape) < 4
    return 0.125 * jnp.where(low, pairs[:, :, 0], pairs[:, :, 1])


def pair_sum(planes):
    pairs = planes.reshape((planes.shape[0] // 2, 2) + planes.shape[1:])
    return pairs[:, 0] + pairs[:, 1]


def twice(planes):
    shape = (planes.shape[0], 2) + planes.shape[1:]
    return jnp.broadcast_to(planes[:, None], shape).reshape((2 * planes.shape[0],) + planes.shape[1:])


def prolong_whole(coarse, depth):
    if depth == 5:
        return twice(sub_take(coarse, lambda s: s // 2))
    low = sub_take(coarse, lambda s: s // 2)
    high = sub_take(coarse, lambda s: 4 + s // 2)
    both = jnp.stack([low, high], axis=2)
    return twice(both.reshape((coarse.shape[0], 2 * coarse.shape[1], 8, 128)))


def loop(count, body):
    def step(i, carry):
        body(i)
        return carry

    lax.fori_loop(0, count, step, 0)


def kernel(rhs, cot, phase, out_a, out_b, *scratch):
    scratch = list(scratch)

    def take(count):
        got = scratch[:count]
        del scratch[:count]
        return got

    zero = Finest(0, take(10))
    one, two = Level(1, take(10)), Level(2, take(10))
    whole = [Level(depth, take(10)) for depth in range(3, 7)]
    answers = take(5)
    phases, staged, rows_m, rows_s = take(4)
    in_sem, out_sem, near_send, near_recv, far_send, far_recv = take(6)
    gy, gz = lax.axis_index("gy"), lax.axis_index("gz")

    def to_z(step):
        return {"gz": lax.rem(gz + step + RING, RING)}

    def to_y(step):
        return {"gy": lax.rem(gy + step + RING, RING)}

    def to(dy, dz):
        return {"gy": lax.rem(gy + dy + RING, RING), "gz": lax.rem(gz + dz + RING, RING)}

    loads = []
    for group, (src, dst, first) in enumerate(((phase, phases, 0), (rhs, zero.src, 0), (cot, zero.src, 4))):
        edge = 3 if group == 0 else 2
        parts = []
        for part in range(4):
            copy = pltpu.make_async_copy(
                src.at[:, :, pl.ds(128 * part, 128)],
                dst.at[pl.ds(edge, 16), pl.ds(edge, 16), first + part],
                in_sem.at[4 * group + part],
            )
            copy.start()
            parts.append(copy)
        loads.append(parts)

    barrier = pltpu.get_barrier_semaphore()
    for dy, dz in ((1, 1), (1, -1), (-1, 1), (-1, -1)):
        pl.semaphore_signal(barrier, inc=1, device_id=to(dy, dz), device_id_type=MESH)

    def greet(i):
        pl.semaphore_signal(barrier, inc=1, device_id=to_z(i + 1), device_id_type=MESH)
        pl.semaphore_signal(barrier, inc=1, device_id=to_y(i + 1), device_id_type=MESH)

    loop(RING - 1, greet)

    for level in whole:
        count = level.val.shape[0]
        blank = jnp.zeros((1,) + level.val.shape[1:], F32)
        for ref in (level.mob, level.val, level.smo, level.err):
            ref[pl.ds(0, 1)] = blank
            ref[pl.ds(count - 1, 1)] = blank
    for level in whole:
        level.az[pl.ds(0, 1)] = jnp.zeros((1,) + level.val.shape[1:], F32)
    for end in (0, 34):
        answers[2][pl.ds(end, 2)] = jnp.zeros((2, 4, 8, 128), F32)

    def inside(position, extent):
        ok = jnp.logical_and(position >= 0, position < extent)
        return jnp.where(ok, 1.0, 0.0).astype(F32)

    def mobility_of(values, mask):
        found = jnp.where(values == 1, HEAVY, LIGHT).astype(F32) * mask
        return sub_take(found, lambda s: s % 4)

    for copy in loads[0]:
        copy.wait()

    def own_mobility(i):
        total = None
        for plane in (0, 1):
            at = 3 + 2 * i + plane
            found = mobility_of(phases[at, pl.ds(3, 16)], 1.0)
            zero.mob[at, pl.ds(3, 16)] = found
            total = found if total is None else total + found
        one.mob[4 + i, pl.ds(2, 4)] = restrict_0(total)

    loop(8, own_mobility)
    two.mob[pl.ds(4, 4), 1] = restrict_1(pair_sum(one.mob[pl.ds(4, 8), pl.ds(2, 4)]))
    rows_m[...] = restrict_2(pair_sum(two.mob[pl.ds(4, 4), 1]))
    for copy in loads[1] + loads[2]:
        copy.wait()

    pl.semaphore_wait(barrier, 4 + 2 * (RING - 1))

    def edges(step, low, size, width):
        if step == 0:
            return low, low, size
        if step == 1:
            return low + size - width, low - width, width
        return low, low + size, width

    def exchange(slot, ref, z_geometry, y_geometry, rows=None):
        copies = []
        for number, (dy, dz) in enumerate(AROUND):
            z_from, z_to, z_count = edges(dz, *z_geometry)
            y_from, y_to, y_count = edges(dy, *y_geometry)
            src = (pl.ds(z_from, z_count), pl.ds(y_from, y_count))
            dst = (pl.ds(z_to, z_count), pl.ds(y_to, y_count))
            if rows is not None:
                src, dst = src + (pl.ds(0, rows),), dst + (pl.ds(0, rows),)
            copy = pltpu.make_async_remote_copy(
                src_ref=ref.at[src],
                dst_ref=ref.at[dst],
                send_sem=near_send.at[slot, number],
                recv_sem=near_recv.at[slot, number],
                device_id=to(dy, dz),
                device_id_type=MESH,
            )
            copy.start()
            copies.append(copy)
        return copies

    def landed(copies):
        for copy in copies:
            copy.wait_recv()

    def place(ref):
        return ref.at[pl.ds(2 * gz + 1, 2), gy // 4, pl.ds(2 * lax.rem(gy, 4), 2)]

    def gather_z(slot, rows, ref):
        own = pltpu.make_async_copy(rows.at[pl.ds(0, 2), pl.ds(0, 2)], place(ref), far_send.at[slot, 2])
        own.start()

        def send(i):
            pltpu.make_async_remote_copy(
                src_ref=rows.at[pl.ds(0, 2), pl.ds(0, 2)],
                dst_ref=place(ref),
                send_sem=far_send.at[slot, 0],
                recv_sem=far_recv.at[slot, 0],
                device_id=to_z(i + 1),
                device_id_type=MESH,
            ).start()

        loop(RING - 1, send)
        return own

    def settle(ref, semaphore, planes):
        part = ref.at[pl.ds(1, planes), 0, pl.ds(0, 2)]
        pltpu.make_async_copy(part, part, semaphore).wait()

    def gather_y(slot, ref, own):
        own.wait()
        settle(ref, far_recv.at[slot, 0], 2 * (RING - 1))
        part = ref.at[pl.ds(1, 32), gy // 4, pl.ds(2 * lax.rem(gy, 4), 2)]

        def send(i):
            pltpu.make_async_remote_copy(
                src_ref=part,
                dst_ref=part,
                send_sem=far_send.at[slot, 1],
                recv_sem=far_recv.at[slot, 1],
                device_id=to_y(i + 1),
                device_id_type=MESH,
            ).start()

        loop(RING - 1, send)

    def drain(ref, semaphore):
        part = ref.at[pl.ds(1, 30)]
        pltpu.make_async_copy(part, part, semaphore).wait()

    sent = []
    phase_halo = exchange(0, phases, (3, 16, 3), (3, 16, 3), 4)
    source_halo = exchange(1, zero.src, (2, 16, 2), (2, 16, 2))
    own_m = gather_z(0, rows_m, whole[0].mob)
    mob_one = exchange(2, one.mob, (4, 8, 4), (2, 4, 2))
    mob_two = exchange(3, two.mob, (4, 4, 4), (1, 1, 1))
    sent += phase_halo + source_halo + mob_one + mob_two

    def z_mask(plane_at, depth, first):
        block = 16 >> depth
        return inside(gz * block + plane_at - first, 256 >> depth)

    landed(phase_halo)

    def outer_mobility(i):
        at = jnp.where(i < 3, i, i + 16)
        mask = z_mask(at, 0, 3)
        zero.mob[at, pl.ds(0, 22)] = mobility_of(phases[at, pl.ds(0, 22)], mask)

    loop(6, outer_mobility)

    def side_mobility(i):
        for first in (0, 19):
            zero.mob[3 + i, pl.ds(first, 3)] = mobility_of(phases[3 + i, pl.ds(first, 3)], 1.0)

    loop(16, side_mobility)

    def coefficients_zero(i):
        for low in (0, 10):
            zero.coefficients(i, low, 10, z_mask(i, 0, 2))

    loop(20, coefficients_zero)
    landed(source_halo)

    def start_zero(i):
        zero.start(i, 0, 20)

    loop(20, start_zero)

    def smooth_zero(i):
        for low in (1, 10):
            zero.smooth(i + 1, low, 9)

    loop(18, smooth_zero)

    for at in (0, 19):
        zero.smo[at] = zero.val[at]

    def ring_zero(i):
        for at in (0, 19):
            zero.smo[i + 1, at] = zero.val[i + 1, at]

    loop(18, ring_zero)

    def remainder_zero(i):
        for half in (0, 1):
            low = 2 + 8 * half
            total = zero.remainder(2 + 2 * i, low, 8) + zero.remainder(3 + 2 * i, low, 8)
            one.src[4 + i, pl.ds(2 + 2 * half, 2)] = restrict_0(total)

    loop(8, remainder_zero)
    source_one = exchange(4, one.src, (4, 8, 3), (2, 4, 2))
    sent += source_one

    gather_y(0, whole[0].mob, own_m)
    landed(mob_one)
    landed(mob_two)

    def fix_mobility(level, planes, depth):
        for at in range(planes):
            level.mob[at] = level.mob[at] * z_mask(at, depth, planes)
            last = level.mob.shape[0] - 1 - at
            level.mob[last] = level.mob[last] * z_mask(last, depth, planes)

    fix_mobility(one, 4, 1)
    fix_mobility(two, 4, 2)

    def masks(at, count, depth, first):
        return jnp.stack([jnp.full((1, 8, 128), z_mask(at + j, depth, first), F32) for j in range(count)])

    def coefficients_one(i):
        at = 1 + 2 * i
        one.inv[pl.ds(at, 2)] = one.coefficients(at, 2, masks(at, 2, 1, 4))

    loop(7, coefficients_one)

    def coefficients_two(i):
        at = 1 + 2 * i
        found = two.coefficients(at, 2, masks(at, 2, 2, 4))
        two.rem[pl.ds(at, 2)] = found

    loop(5, coefficients_two)
    two.az[0] = two.scale * (two.mob[0] + two.mob[1])
    two.inv[pl.ds(4, 4), 1] = two.rem[pl.ds(4, 4), 1]
    inverse_two = exchange(5, two.inv, (4, 4, 4), (1, 1, 1))
    sent += inverse_two

    landed(source_one)

    def start_one(i):
        one.start(1 + 2 * i, 2)

    loop(7, start_one)

    def smooth_one(i):
        one.smooth(2 + 2 * i, 2)

    loop(6, smooth_one)
    for at in (1, 14):
        one.smo[at] = one.val[at]

    def remainder_one(i):
        rest = one.remainder(4 + 2 * i, 2)[:, 2:6]
        two.src[pl.ds(4 + i, 1), 1] = restrict_1(pair_sum(rest))[0:1]

    loop(4, remainder_one)
    source_two = exchange(6, two.src, (4, 4, 4), (1, 1, 1))
    sent += source_two

    landed(inverse_two)
    for at in (0, 1, 2, 3, 8, 9, 10, 11):
        two.inv[at] = two.inv[at] * z_mask(at, 2, 4)
    landed(source_two)
    for at in (0, 4, 8):
        two.start(at, 4)
    two.smooth(2, 4)
    two.smooth(6, 4)
    for at in (0, 1, 10, 11):
        two.smo[at] = two.val[at]
    rows_s[...] = restrict_2(pair_sum(two.remainder(4, 4)[:, 1]))
    own_s = gather_z(1, rows_s, whole[0].src)

    drain(whole[0].mob, far_recv.at[0, 1])

    block = (4, 8, 8, 4)
    steps = (8, 2, 1, 1)
    for number, level in enumerate(whole):
        size = block[number]
        if number > 0:
            finer = whole[number - 1]

            def coarsen(i, finer=finer, level=level, size=size, number=number):
                total = pair_sum(finer.mob[pl.ds(1 + 2 * size * i, 2 * size)])
                level.mob[pl.ds(1 + size * i, size)] = restrict_whole(total, number + 2)

            loop(steps[number], coarsen)

        level.az[pl.ds(0, 1)] = level.scale * level.mob[pl.ds(1, 1)]

        def coefficients(i, level=level, size=size):
            at = 1 + size * i
            level.inv[pl.ds(at, size)] = level.coefficients(at, size)

        loop(steps[number], coefficients)

    gather_y(1, whole[0].src, own_s)
    drain(whole[0].src, far_recv.at[1, 1])

    for number, level in enumerate(whole[:-1]):
        size = block[number]
        coarser = whole[number + 1]

        def start(i, level=level, size=size):
            level.start(1 + size * i, size)

        def smooth(i, level=level, size=size):
            level.smooth(1 + size * i, size)

        def lower(i, level=level, size=size, coarser=coarser, number=number):
            rest = pair_sum(level.remainder(1 + size * i, size))
            coarser.src[pl.ds(1 + (size // 2) * i, size // 2)] = restrict_whole(rest, number + 3)

        loop(steps[number], start)
        loop(steps[number], smooth)
        loop(steps[number], lower)

    last = whole[-1]
    last.start(1, 4)
    iterate = last.val[pl.ds(1, 4)]
    direction = iterate
    factor = FIRST
    for _ in range(3):
        _, applied = last.operate(last.val, 1, 4)
        following = 1.0 / (2.0 * RATIO - factor)
        rest = last.src[pl.ds(1, 4)] - applied
        direction = (following * factor) * direction + (2.0 * following / HALF) * (last.inv[pl.ds(1, 4)] * rest)
        iterate = iterate + direction
        last.val[pl.ds(1, 4)] = iterate
        factor = following
    coarse, offset = last.val, 1

    for number in (2, 1, 0):
        level = whole[number]
        size = block[number]
        target, shift = ((answers[2], 2), (answers[3], 0), (answers[4], 0))[number]

        def add(i, level=level, size=size, coarse=coarse, offset=offset, number=number):
            part = coarse[pl.ds(offset + (size // 2) * i, size // 2)]
            at = 1 + size * i
            level.val[pl.ds(at, size)] = level.smo[pl.ds(at, size)] + prolong_whole(part, number + 3)

        def correct(i, level=level, size=size):
            level.correct(1 + size * i, size)

        def finish(i, level=level, size=size, target=target, shift=shift):
            target[pl.ds(shift + size * i, size)] = level.finish(1 + size * i, size)

        loop(steps[number], add)
        loop(steps[number], correct)
        loop(steps[number], finish)
        coarse, offset = target, shift

    for pair in range(6):
        parts = []
        for tile in range(3):
            row = 2 * lax.rem(gy - 1 + tile + RING, RING)
            found = answers[2][2 * gz + pair, row // 8]
            found = sub_take(found, lambda s, row=row: lax.rem(row, 8) + s // 4)
            parts.append(lane_take(found, lambda s, l: (s % 2) * 64 + l // 2))
        found = jnp.stack(parts)
        for plane in (2 * pair, 2 * pair + 1):
            two.val[plane] = two.smo[plane] + found
    for at in (1, 6):
        two.correct(at, 5)
    for at in (2, 6):
        answers[1][pl.ds(at, 4)] = two.finish(at, 4)

    def add_one(i):
        for half in (0, 1):
            plane = 1 + 2 * i + half
            parts = []
            for tile in range(8):
                at = tile + 2
                found = sub_take(answers[1][(plane + 4) // 2, at // 4], lambda s, at=at: (at % 4) * 2 + (s // 2) % 2)
                parts.append(lane_take(found, lambda s, l: 64 * (s % 2) + l // 2))
            one.val[plane] = one.smo[plane] + jnp.stack(parts)

    loop(7, add_one)

    def correct_one(i):
        one.correct(2 + 2 * i, 2)

    loop(6, correct_one)

    def finish_one(i):
        answers[0][pl.ds(3 + 2 * i, 2)] = one.finish(3 + 2 * i, 2)

    loop(5, finish_one)

    def add_zero(i):
        parts = []
        for pair in range(10):
            at = pair + 3
            found = sub_take(
                answers[0][i + 3, at // 2],
                lambda s, at=at: (at % 2) * 4 + (s // 4) * 2 + (s % 4) // 2,
            )
            found = lane_take(found, lambda s, l: 64 * (s % 2) + l // 2)
            parts += [found, found]
        added = jnp.stack(parts)
        for plane in (0, 1):
            zero.val[2 * i + plane] = zero.smo[2 * i + plane] + added

    loop(10, add_zero)

    def correct_zero(i):
        for low in (1, 10):
            zero.correct(i + 1, low, 9)

    loop(18, correct_zero)

    def finish_zero(i):
        for low in (2, 10):
            staged[i, pl.ds(low - 2, 8)] = zero.finish(i + 2, low, 8)

    loop(16, finish_zero)

    stores = []
    for group, dst in enumerate((out_a, out_b)):
        for part in range(4):
            copy = pltpu.make_async_copy(
                staged.at[:, :, 4 * group + part], dst.at[:, :, pl.ds(128 * part, 128)], out_sem.at[4 * group + part]
            )
            copy.start()
            stores.append(copy)
    for copy in sent:
        copy.wait_send()
    for slot, ref in ((0, whole[0].mob), (1, whole[0].src)):
        settle(ref, far_send.at[slot, 0], 2 * (RING - 1))
        drain(ref, far_send.at[slot, 1])
    for copy in stores:
        copy.wait()


def scratch_shapes():
    shapes = []

    def arrays(planes, tiles, count=10):
        for _ in range(count):
            shapes.append(pltpu.VMEM((planes, tiles, 8, 128), F32))

    arrays(22, 22, 1)
    arrays(20, 20, 9)
    arrays(16, 8)
    arrays(12, 3)
    for planes, tiles in ((34, 4), (18, 2), (10, 1), (6, 1)):
        arrays(planes, tiles)
    arrays(16, 8, 1)
    arrays(12, 3, 1)
    arrays(36, 4, 1)
    arrays(16, 2, 1)
    arrays(8, 1, 1)
    shapes.append(pltpu.VMEM((22, 22, 8, 128), jnp.int32))
    arrays(16, 16, 1)
    shapes.append(pltpu.VMEM((2, 8, 128), F32))
    shapes.append(pltpu.VMEM((2, 8, 128), F32))
    dma = pltpu.SemaphoreType.DMA
    shapes += [dma((12,)), dma((8,)), dma((7, 8)), dma((7, 8)), dma((2, 3)), dma((2, 2))]
    return shapes


def per_device(right_side, cotangent, phase):
    shape = jax.ShapeDtypeStruct(right_side.shape, F32)
    return pl.pallas_call(
        kernel,
        out_shape=(shape, shape),
        in_specs=[pl.BlockSpec(memory_space=pl.ANY)] * 3,
        out_specs=(pl.BlockSpec(memory_space=pl.ANY),) * 2,
        scratch_shapes=scratch_shapes(),
        compiler_params=pltpu.CompilerParams(
            collective_id=0, has_side_effects=True, vmem_limit_bytes=48 * 2**20
        ),
    )(right_side, cotangent, phase)


def solution(mesh):
    spec = P("gz", "gy", None)
    return jax.shard_map(
        per_device, mesh=mesh, in_specs=(spec,) * 3, out_specs=(spec,) * 2, check_vma=False
    )
```

profile of v0, /device:TPU:28, one launch (start us, length us, event | category | flops | bytes accessed | tf_op | source)
XLA Modules:
  0.0 83.2 jit_solution(14308610870436417269)
XLA Ops:
  0.6 0.0 copy-start
  0.6 1.0 %copy-done = f32[16,16,512]{2,1,0:T(8,128)S(1)} copy-done((f32[16,16,512]{2,1,0:T(8,128)S(1)}, f32[16,16,512]{2,1,0:T(8,128)}, u32[]{:S(2)}) %copy-start) | copy-done | bytes 524312
  1.7 0.0 copy-start.1
  1.7 1.0 %copy-done.1 = f32[16,16,512]{2,1,0:T(8,128)S(1)} copy-done((f32[16,16,512]{2,1,0:T(8,128)S(1)}, f32[16,16,512]{2,1,0:T(8,128)}, u32[]{:S(2)}) %copy-start.1) | copy-done | bytes 524312
  2.7 0.0 copy-start.2
  2.7 1.0 %copy-done.2 = s32[16,16,512]{2,1,0:T(8,128)S(1)} copy-done((s32[16,16,512]{2,1,0:T(8,128)S(1)}, s32[16,16,512]{2,1,0:T(8,128)}, u32[]{:S(2)}) %copy-start.2) | copy-done | bytes 524312
  3.8 77.8 %shard_map.50 = (f32[16,16,512]{2,1,0:T(8,128)S(1)}, f32[16,16,512]{2,1,0:T(8,128)S(1)}) custom-call(f32[16,16,512]{2,1,0:T(8,128)S(1)} %copy-done, f32[16,16,512]{2,1,0:T(8,128)S(1)} %copy-done.1, s32[16,16,512]{2,1,0:T(8,128)S(1)} %copy-done.2), custom_call_target="tpu_custom_call" | custom-call | tf_op jit(solution)/shard_map/pallas_call | solution.py:775
  81.6 0.8 copy.7
  82.4 0.8 copy.8
Async XLA Ops:
  0.6 1.0 %copy-start = (f32[16,16,512]{2,1,0:T(8,128)S(1)}, f32[16,16,512]{2,1,0:T(8,128)}, u32[]{:S(2)}) copy-start(f32[16,16,512]{2,1,0:T(8,128)} %rhs.1) | copy-start | bytes 1572868
  1.7 1.0 %copy-start.1 = (f32[16,16,512]{2,1,0:T(8,128)S(1)}, f32[16,16,512]{2,1,0:T(8,128)}, u32[]{:S(2)}) copy-start(f32[16,16,512]{2,1,0:T(8,128)} %cot.1) | copy-start | bytes 1572868
  2.7 1.0 %copy-start.2 = (s32[16,16,512]{2,1,0:T(8,128)S(1)}, s32[16,16,512]{2,1,0:T(8,128)}, u32[]{:S(2)}) copy-start(s32[16,16,512]{2,1,0:T(8,128)} %phase.1) | copy-start | bytes 1572868
where the time goes:
time: 83.4 us; the launch traced here: 83.2 us
  Pallas kernels  77.8 us (93%)
  local copies, waits for them, and re-layouts  4.71 us (6%)
    pallas_call x1, Pallas kernels, per_device(): pl.pallas_call(kernel, out_shape=(shape, shape), in_specs=[pl.BlockSpec(m...  77.8 us
    unnamed x8, local copies, waits for them, and re-layouts  4.71 us

commit v1 on v0

--- a/solution.py
+++ b/solution.py
@@ -64,7 +64,7 @@
     def __init__(self, depth, refs):
         self.depth = depth
         self.scale = 0.5 * 0.25**depth
-        self.mob, self.src, self.az, self.ay, self.ax, self.inv, self.val, self.smo, self.err, self.rem = refs
+        self.mob, self.src, self.az, self.ay, self.ax, self.bx, self.inv, self.val, self.smo, self.err, self.rem = refs
 
     def field_one(self, shape):
         if self.depth == 0:
@@ -108,10 +108,12 @@
         down = self.scale * (here + self.mob[pl.ds(at - 1, count)])
         right = self.scale * (here + self.y_side(here, 1))
         ahead = self.scale * (here + self.x_side(here, 1))
-        diagonal = up + down + right + self.y_side(right, -1) + ahead + self.x_side(ahead, -1)
+        behind = self.scale * (here + self.x_side(here, -1))
+        diagonal = up + down + right + self.y_side(right, -1) + ahead + behind
         self.az[pl.ds(at, count)] = up
         self.ay[pl.ds(at, count)] = right
         self.ax[pl.ds(at, count)] = ahead
+        self.bx[pl.ds(at, count)] = behind
         return self.masked_inverse(diagonal, mask)
 
     def masked_inverse(self, diagonal, mask):
@@ -125,8 +127,8 @@
         total = total + self.az[pl.ds(at - 1, count)] * (here - ref[pl.ds(at - 1, count)])
         flux = self.ay[pl.ds(at, count)] * (here - self.y_side(here, 1))
         total = total + (flux - self.y_side(flux, -1))
-        flux = self.ax[pl.ds(at, count)] * (here - self.x_side(here, 1))
-        return here, total + (flux - self.x_side(flux, -1))
+        total = total + self.ax[pl.ds(at, count)] * (here - self.x_side(here, 1))
+        return here, total + self.bx[pl.ds(at, count)] * (here - self.x_side(here, -1))
 
     def start(self, at, count):
         self.val[pl.ds(at, count)] = self.src[pl.ds(at, count)] * self.inv[pl.ds(at, count)] * (1.0 / MID)
@@ -163,10 +165,12 @@
         down = self.scale * (mid + self.mob[plane, pl.ds(low + 1, count)])
         right = self.scale * (here[:-1] + here[1:])
         ahead = self.scale * (mid + self.x_side(mid, 1))
-        diagonal = up + down + right[1:] + right[:-1] + ahead + self.x_side(ahead, -1)
+        behind = self.scale * (mid + self.x_side(mid, -1))
+        diagonal = up + down + right[1:] + right[:-1] + ahead + behind
         self.az[plane, pl.ds(low, count)] = up
         self.ay[plane, pl.ds(low, count)] = right[1:]
         self.ax[plane, pl.ds(low, count)] = ahead
+        self.bx[plane, pl.ds(low, count)] = behind
         self.inv[plane, pl.ds(low, count)] = self.masked_inverse(diagonal, mask)
 
     def operate(self, ref, plane, low, count):
@@ -177,8 +181,8 @@
         total = total + self.az[plane - 1, part] * (here - ref[plane - 1, part])
         flux = self.ay[plane, pl.ds(low - 1, count + 1)] * (wide[:-1] - wide[1:])
         total = total + (flux[1:] - flux[:-1])
-        flux = self.ax[plane, part] * (here - self.x_side(here, 1))
-        return here, total + (flux - self.x_side(flux, -1))
+        total = total + self.ax[plane, part] * (here - self.x_side(here, 1))
+        return here, total + self.bx[plane, part] * (here - self.x_side(here, -1))
 
     def start(self, plane, low, count):
         part = pl.ds(low, count)
@@ -212,7 +216,7 @@
 
 
 def halves(values):
-    return lane_take(values + lane_roll(values, -1), lambda s, l: (2 * l) % 128)
+    return lane_take(values, lambda s, l: (2 * l) % 128) + lane_take(values, lambda s, l: (2 * l + 1) % 128)
 
 
 def restrict_0(planes):
@@ -276,12 +280,12 @@
     return twice(both.reshape((coarse.shape[0], 2 * coarse.shape[1], 8, 128)))
 
 
-def loop(count, body):
+def loop(count, body, unroll=1):
     def step(i, carry):
         body(i)
         return carry
 
-    lax.fori_loop(0, count, step, 0)
+    lax.fori_loop(0, count, step, 0, unroll=unroll)
 
 
 def kernel(rhs, cot, phase, out_a, out_b, *scratch):
@@ -292,12 +296,12 @@
         del scratch[:count]
         return got
 
-    zero = Finest(0, take(10))
-    one, two = Level(1, take(10)), Level(2, take(10))
-    whole = [Level(depth, take(10)) for depth in range(3, 7)]
+    zero = Finest(0, take(11))
+    one, two = Level(1, take(11)), Level(2, take(11))
+    whole = [Level(depth, take(11)) for depth in range(3, 7)]
     answers = take(5)
     phases, staged, rows_m, rows_s = take(4)
-    in_sem, out_sem, near_send, near_recv, far_send, far_recv = take(6)
+    in_sem, out_sem, near_send, near_recv, far_send, far_recv, known = take(7)
     gy, gz = lax.axis_index("gy"), lax.axis_index("gz")
 
     def to_z(step):
@@ -324,14 +328,8 @@
         loads.append(parts)
 
     barrier = pltpu.get_barrier_semaphore()
-    for dy, dz in ((1, 1), (1, -1), (-1, 1), (-1, -1)):
+    for dy, dz in AROUND:
         pl.semaphore_signal(barrier, inc=1, device_id=to(dy, dz), device_id_type=MESH)
-
-    def greet(i):
-        pl.semaphore_signal(barrier, inc=1, device_id=to_z(i + 1), device_id_type=MESH)
-        pl.semaphore_signal(barrier, inc=1, device_id=to_y(i + 1), device_id_type=MESH)
-
-    loop(RING - 1, greet)
 
     for level in whole:
         count = level.val.shape[0]
@@ -364,13 +362,20 @@
             total = found if total is None else total + found
         one.mob[4 + i, pl.ds(2, 4)] = restrict_0(total)
 
-    loop(8, own_mobility)
+    loop(8, own_mobility, 2)
     two.mob[pl.ds(4, 4), 1] = restrict_1(pair_sum(one.mob[pl.ds(4, 8), pl.ds(2, 4)]))
     rows_m[...] = restrict_2(pair_sum(two.mob[pl.ds(4, 4), 1]))
     for copy in loads[1] + loads[2]:
         copy.wait()
 
-    pl.semaphore_wait(barrier, 4 + 2 * (RING - 1))
+    pl.semaphore_wait(barrier, len(AROUND))
+
+    def tell(number):
+        away = 2**number
+        for device in (to_z(away), to_z(-away), to_y(away), to_y(-away)):
+            pl.semaphore_signal(known.at[number], inc=1, device_id=device, device_id_type=MESH)
+
+    tell(0)
 
     def edges(step, low, size, width):
         if step == 0:
@@ -452,9 +457,13 @@
     sent = []
     phase_halo = exchange(0, phases, (3, 16, 3), (3, 16, 3), 4)
     source_halo = exchange(1, zero.src, (2, 16, 2), (2, 16, 2))
-    own_m = gather_z(0, rows_m, whole[0].mob)
     mob_one = exchange(2, one.mob, (4, 8, 4), (2, 4, 2))
     mob_two = exchange(3, two.mob, (4, 4, 4), (1, 1, 1))
+    for number in range(3):
+        pl.semaphore_wait(known.at[number], 4)
+        if number < 2:
+            tell(number + 1)
+    own_m = gather_z(0, rows_m, whole[0].mob)
     sent += phase_halo + source_halo + mob_one + mob_two
 
     def z_mask(plane_at, depth, first):
@@ -468,31 +477,31 @@
         mask = z_mask(at, 0, 3)
         zero.mob[at, pl.ds(0, 22)] = mobility_of(phases[at, pl.ds(0, 22)], mask)
 
-    loop(6, outer_mobility)
+    loop(6, outer_mobility, 2)
 
     def side_mobility(i):
         for first in (0, 19):
             zero.mob[3 + i, pl.ds(first, 3)] = mobility_of(phases[3 + i, pl.ds(first, 3)], 1.0)
 
-    loop(16, side_mobility)
+    loop(16, side_mobility, 4)
 
     def coefficients_zero(i):
         for low in (0, 10):
             zero.coefficients(i, low, 10, z_mask(i, 0, 2))
 
-    loop(20, coefficients_zero)
+    loop(20, coefficients_zero, 2)
     landed(source_halo)
 
     def start_zero(i):
         zero.start(i, 0, 20)
 
-    loop(20, start_zero)
+    loop(20, start_zero, 2)
 
     def smooth_zero(i):
         for low in (1, 10):
             zero.smooth(i + 1, low, 9)
 
-    loop(18, smooth_zero)
+    loop(18, smooth_zero, 3)
 
     for at in (0, 19):
         zero.smo[at] = zero.val[at]
@@ -501,7 +510,7 @@
         for at in (0, 19):
             zero.smo[i + 1, at] = zero.val[i + 1, at]
 
-    loop(18, ring_zero)
+    loop(18, ring_zero, 6)
 
     def remainder_zero(i):
         for half in (0, 1):
@@ -509,7 +518,7 @@
             total = zero.remainder(2 + 2 * i, low, 8) + zero.remainder(3 + 2 * i, low, 8)
             one.src[4 + i, pl.ds(2 + 2 * half, 2)] = restrict_0(total)
 
-    loop(8, remainder_zero)
+    loop(8, remainder_zero, 2)
     source_one = exchange(4, one.src, (4, 8, 3), (2, 4, 2))
     sent += source_one
 
@@ -533,14 +542,14 @@
         at = 1 + 2 * i
         one.inv[pl.ds(at, 2)] = one.coefficients(at, 2, masks(at, 2, 1, 4))
 
-    loop(7, coefficients_one)
+    loop(7, coefficients_one, 7)
 
     def coefficients_two(i):
         at = 1 + 2 * i
         found = two.coefficients(at, 2, masks(at, 2, 2, 4))
         two.rem[pl.ds(at, 2)] = found
 
-    loop(5, coefficients_two)
+    loop(5, coefficients_two, 5)
     two.az[0] = two.scale * (two.mob[0] + two.mob[1])
     two.inv[pl.ds(4, 4), 1] = two.rem[pl.ds(4, 4), 1]
     inverse_two = exchange(5, two.inv, (4, 4, 4), (1, 1, 1))
@@ -551,12 +560,12 @@
     def start_one(i):
         one.start(1 + 2 * i, 2)
 
-    loop(7, start_one)
+    loop(7, start_one, 7)
 
     def smooth_one(i):
         one.smooth(2 + 2 * i, 2)
 
-    loop(6, smooth_one)
+    loop(6, smooth_one, 6)
     for at in (1, 14):
         one.smo[at] = one.val[at]
 
@@ -564,7 +573,7 @@
         rest = one.remainder(4 + 2 * i, 2)[:, 2:6]
         two.src[pl.ds(4 + i, 1), 1] = restrict_1(pair_sum(rest))[0:1]
 
-    loop(4, remainder_one)
+    loop(4, remainder_one, 4)
     source_two = exchange(6, two.src, (4, 4, 4), (1, 1, 1))
     sent += source_two
 
@@ -594,7 +603,7 @@
                 total = pair_sum(finer.mob[pl.ds(1 + 2 * size * i, 2 * size)])
                 level.mob[pl.ds(1 + size * i, size)] = restrict_whole(total, number + 2)
 
-            loop(steps[number], coarsen)
+            loop(steps[number], coarsen, steps[number])
 
         level.az[pl.ds(0, 1)] = level.scale * level.mob[pl.ds(1, 1)]
 
@@ -602,7 +611,7 @@
             at = 1 + size * i
             level.inv[pl.ds(at, size)] = level.coefficients(at, size)
 
-        loop(steps[number], coefficients)
+        loop(steps[number], coefficients, steps[number])
 
     gather_y(1, whole[0].src, own_s)
     drain(whole[0].src, far_recv.at[1, 1])
@@ -621,9 +630,9 @@
             rest = pair_sum(level.remainder(1 + size * i, size))
             coarser.src[pl.ds(1 + (size // 2) * i, size // 2)] = restrict_whole(rest, number + 3)
 
-        loop(steps[number], start)
-        loop(steps[number], smooth)
-        loop(steps[number], lower)
+        loop(steps[number], start, steps[number])
+        loop(steps[number], smooth, steps[number])
+        loop(steps[number], lower, steps[number])
 
     last = whole[-1]
     last.start(1, 4)
@@ -656,9 +665,9 @@
         def finish(i, level=level, size=size, target=target, shift=shift):
             target[pl.ds(shift + size * i, size)] = level.finish(1 + size * i, size)
 
-        loop(steps[number], add)
-        loop(steps[number], correct)
-        loop(steps[number], finish)
+        loop(steps[number], add, steps[number])
+        loop(steps[number], correct, steps[number])
+        loop(steps[number], finish, steps[number])
         coarse, offset = target, shift
 
     for pair in range(6):
@@ -686,17 +695,17 @@
                 parts.append(lane_take(found, lambda s, l: 64 * (s % 2) + l // 2))
             one.val[plane] = one.smo[plane] + jnp.stack(parts)
 
-    loop(7, add_one)
+    loop(7, add_one, 7)
 
     def correct_one(i):
         one.correct(2 + 2 * i, 2)
 
-    loop(6, correct_one)
+    loop(6, correct_one, 6)
 
     def finish_one(i):
         answers[0][pl.ds(3 + 2 * i, 2)] = one.finish(3 + 2 * i, 2)
 
-    loop(5, finish_one)
+    loop(5, finish_one, 5)
 
     def add_zero(i):
         parts = []
@@ -712,19 +721,19 @@
         for plane in (0, 1):
             zero.val[2 * i + plane] = zero.smo[2 * i + plane] + added
 
-    loop(10, add_zero)
+    loop(10, add_zero, 2)
 
     def correct_zero(i):
         for low in (1, 10):
             zero.correct(i + 1, low, 9)
 
-    loop(18, correct_zero)
+    loop(18, correct_zero, 3)
 
     def finish_zero(i):
         for low in (2, 10):
             staged[i, pl.ds(low - 2, 8)] = zero.finish(i + 2, low, 8)
 
-    loop(16, finish_zero)
+    loop(16, finish_zero, 4)
 
     stores = []
     for group, dst in enumerate((out_a, out_b)):
@@ -746,12 +755,12 @@
 def scratch_shapes():
     shapes = []
 
-    def arrays(planes, tiles, count=10):
+    def arrays(planes, tiles, count=11):
         for _ in range(count):
             shapes.append(pltpu.VMEM((planes, tiles, 8, 128), F32))
 
     arrays(22, 22, 1)
-    arrays(20, 20, 9)
+    arrays(20, 20, 10)
     arrays(16, 8)
     arrays(12, 3)
     for planes, tiles in ((34, 4), (18, 2), (10, 1), (6, 1)):
@@ -766,7 +775,7 @@
     shapes.append(pltpu.VMEM((2, 8, 128), F32))
     shapes.append(pltpu.VMEM((2, 8, 128), F32))
     dma = pltpu.SemaphoreType.DMA
-    shapes += [dma((12,)), dma((8,)), dma((7, 8)), dma((7, 8)), dma((2, 3)), dma((2, 2))]
+    shapes += [dma((12,)), dma((8,)), dma((7, 8)), dma((7, 8)), dma((2, 3)), dma((2, 2)), pltpu.SemaphoreType.REGULAR((3,))]
     return shapes
 
 
@@ -779,7 +788,7 @@
         out_specs=(pl.BlockSpec(memory_space=pl.ANY),) * 2,
         scratch_shapes=scratch_shapes(),
         compiler_params=pltpu.CompilerParams(
-            collective_id=0, has_side_effects=True, vmem_limit_bytes=48 * 2**20
+            collective_id=0, has_side_effects=True, vmem_limit_bytes=62 * 2**20
         ),
     )(right_side, cotangent, phase)
 

time: 83.4 us -> 64 us (0.77)
  the two profiles are of different devices: /device:TPU:28 before, /device:TPU:1 now
where the time goes in v1:
time: 64 us; the launch traced here: 63.8 us
  Pallas kernels  60.5 us (95%)
  local copies, waits for them, and re-layouts  2.74 us (4%)
  between operations  0.65 us (1%)
    pallas_call x1, Pallas kernels, per_device(): pl.pallas_call(kernel, out_shape=(shape, shape), in_specs=[pl.BlockSpec(m...  60.5 us
    unnamed x4, local copies, waits for them, and re-layouts  2.74 us

profile of v1, /device:TPU:1, one launch (start us, length us, event | category | flops | bytes accessed | tf_op | source)
XLA Modules:
  0.0 63.8 jit_solution(12857691550649666157)
XLA Ops:
  0.6 60.5 %shard_map.50 = (f32[16,16,512]{2,1,0:T(8,128)}, f32[16,16,512]{2,1,0:T(8,128)}) custom-call(f32[16,16,512]{2,1,0:T(8,128)} %rhs.1, f32[16,16,512]{2,1,0:T(8,128)} %cot.1, s32[16,16,512]{2,1,0:T(8,128)} %phase.1), custom_call_target="tpu_custom_call" | custom-call | tf_op jit(solution)/shard_map/pallas_call | solution.py:784
  61.1 0.0 copy-start
  61.1 1.9 %copy.7 = f32[16,16,512]{2,1,0:T(8,128)} copy(f32[16,16,512]{2,1,0:T(8,128)} %get-tuple-element.4) | data formatting | bytes 1048576
  63.0 0.0 copy-done
  63.0 0.8 %copy.8 = f32[16,16,512]{2,1,0:T(8,128)} copy(f32[16,16,512]{2,1,0:T(8,128)S(1)} %copy-done) | data formatting | bytes 1048576
Async XLA Ops:
  61.1 2.0 %copy-start = (f32[16,16,512]{2,1,0:T(8,128)S(1)}, f32[16,16,512]{2,1,0:T(8,128)}, u32[]{:S(2)}) copy-start(f32[16,16,512]{2,1,0:T(8,128)} %get-tuple-element.5) | copy-start | bytes 1572868

commit v2 on v1

--- a/solution.py
+++ b/solution.py
@@ -18,7 +18,9 @@
 C2 = 2.0 * SECOND / HALF
 LIGHT = 1.0
 HEAVY = 1.0 / 8.0
-AROUND = tuple((a, b) for a in (-1, 0, 1) for b in (-1, 0, 1) if (a, b) != (0, 0))
+AROUND = ((1, 1), (1, -1), (-1, 1), (-1, -1), (1, 0), (-1, 0), (0, 1), (0, -1))
+FAR_Z = (8, 7, 9, 6, 10, 5, 11, 4, 12, 3, 13, 2, 14, 1, 15)
+FAR_Y = (10, 6, 9, 11, 14, 7, 5, 13, 2, 8, 15, 1, 3, 12, 4)
 F32 = jnp.float32
 
 
@@ -171,7 +173,9 @@
         self.ay[plane, pl.ds(low, count)] = right[1:]
         self.ax[plane, pl.ds(low, count)] = ahead
         self.bx[plane, pl.ds(low, count)] = behind
-        self.inv[plane, pl.ds(low, count)] = self.masked_inverse(diagonal, mask)
+        inverse = self.masked_inverse(diagonal, mask)
+        self.inv[plane, pl.ds(low, count)] = inverse
+        self.val[plane, pl.ds(low, count)] = self.src[plane, pl.ds(low, count)] * inverse * (1.0 / MID)
 
     def operate(self, ref, plane, low, count):
         wide = ref[plane, pl.ds(low - 1, count + 2)]
@@ -183,10 +187,6 @@
         total = total + (flux[1:] - flux[:-1])
         total = total + self.ax[plane, part] * (here - self.x_side(here, 1))
         return here, total + self.bx[plane, part] * (here - self.x_side(here, -1))
-
-    def start(self, plane, low, count):
-        part = pl.ds(low, count)
-        self.val[plane, part] = self.src[plane, part] * self.inv[plane, part] * (1.0 / MID)
 
     def smooth(self, plane, low, count):
         part = pl.ds(low, count)
@@ -350,24 +350,8 @@
         found = jnp.where(values == 1, HEAVY, LIGHT).astype(F32) * mask
         return sub_take(found, lambda s: s % 4)
 
-    for copy in loads[0]:
+    for copy in loads[0] + loads[1] + loads[2]:
         copy.wait()
-
-    def own_mobility(i):
-        total = None
-        for plane in (0, 1):
-            at = 3 + 2 * i + plane
-            found = mobility_of(phases[at, pl.ds(3, 16)], 1.0)
-            zero.mob[at, pl.ds(3, 16)] = found
-            total = found if total is None else total + found
-        one.mob[4 + i, pl.ds(2, 4)] = restrict_0(total)
-
-    loop(8, own_mobility, 2)
-    two.mob[pl.ds(4, 4), 1] = restrict_1(pair_sum(one.mob[pl.ds(4, 8), pl.ds(2, 4)]))
-    rows_m[...] = restrict_2(pair_sum(two.mob[pl.ds(4, 4), 1]))
-    for copy in loads[1] + loads[2]:
-        copy.wait()
-
     pl.semaphore_wait(barrier, len(AROUND))
 
     def tell(number):
@@ -416,17 +400,15 @@
         own = pltpu.make_async_copy(rows.at[pl.ds(0, 2), pl.ds(0, 2)], place(ref), far_send.at[slot, 2])
         own.start()
 
-        def send(i):
+        for away in FAR_Z:
             pltpu.make_async_remote_copy(
                 src_ref=rows.at[pl.ds(0, 2), pl.ds(0, 2)],
                 dst_ref=place(ref),
                 send_sem=far_send.at[slot, 0],
                 recv_sem=far_recv.at[slot, 0],
-                device_id=to_z(i + 1),
+                device_id=to_z(away),
                 device_id_type=MESH,
             ).start()
-
-        loop(RING - 1, send)
         return own
 
     def settle(ref, semaphore, planes):
@@ -438,17 +420,15 @@
         settle(ref, far_recv.at[slot, 0], 2 * (RING - 1))
         part = ref.at[pl.ds(1, 32), gy // 4, pl.ds(2 * lax.rem(gy, 4), 2)]
 
-        def send(i):
+        for away in FAR_Y:
             pltpu.make_async_remote_copy(
                 src_ref=part,
                 dst_ref=part,
                 send_sem=far_send.at[slot, 1],
                 recv_sem=far_recv.at[slot, 1],
-                device_id=to_y(i + 1),
+                device_id=to_y(away),
                 device_id_type=MESH,
             ).start()
-
-        loop(RING - 1, send)
 
     def drain(ref, semaphore):
         part = ref.at[pl.ds(1, 30)]
@@ -457,19 +437,42 @@
     sent = []
     phase_halo = exchange(0, phases, (3, 16, 3), (3, 16, 3), 4)
     source_halo = exchange(1, zero.src, (2, 16, 2), (2, 16, 2))
+    def own_mobility(i):
+        total = None
+        for plane in (0, 1):
+            at = 3 + 2 * i + plane
+            found = mobility_of(phases[at, pl.ds(3, 16)], 1.0)
+            zero.mob[at, pl.ds(3, 16)] = found
+            total = found if total is None else total + found
+        one.mob[4 + i, pl.ds(2, 4)] = restrict_0(total)
+
+    loop(8, own_mobility, 2)
+    two.mob[pl.ds(4, 4), 1] = restrict_1(pair_sum(one.mob[pl.ds(4, 8), pl.ds(2, 4)]))
+    rows_m[...] = restrict_2(pair_sum(two.mob[pl.ds(4, 4), 1]))
     mob_one = exchange(2, one.mob, (4, 8, 4), (2, 4, 2))
     mob_two = exchange(3, two.mob, (4, 4, 4), (1, 1, 1))
-    for number in range(3):
-        pl.semaphore_wait(known.at[number], 4)
-        if number < 2:
-            tell(number + 1)
-    own_m = gather_z(0, rows_m, whole[0].mob)
     sent += phase_halo + source_halo + mob_one + mob_two
 
     def z_mask(plane_at, depth, first):
         block = 16 >> depth
         return inside(gz * block + plane_at - first, 256 >> depth)
 
+    pl.semaphore_wait(known.at[0], 4)
+    tell(1)
+
+    def inner_coefficients(i):
+        zero.coefficients(3 + i, 3, 14, None)
+
+    loop(14, inner_coefficients, 2)
+    pl.semaphore_wait(known.at[1], 4)
+    tell(2)
+
+    def inner_smooth(i):
+        zero.smooth(4 + i, 4, 12)
+
+    loop(12, inner_smooth, 3)
+    pl.semaphore_wait(known.at[2], 4)
+    own_m = gather_z(0, rows_m, whole[0].mob)
     landed(phase_halo)
 
     def outer_mobility(i):
@@ -485,23 +488,30 @@
 
     loop(16, side_mobility, 4)
 
-    def coefficients_zero(i):
-        for low in (0, 10):
-            zero.coefficients(i, low, 10, z_mask(i, 0, 2))
-
-    loop(20, coefficients_zero, 2)
     landed(source_halo)
 
-    def start_zero(i):
-        zero.start(i, 0, 20)
-
-    loop(20, start_zero, 2)
-
-    def smooth_zero(i):
-        for low in (1, 10):
-            zero.smooth(i + 1, low, 9)
-
-    loop(18, smooth_zero, 3)
+    def outer_coefficients(i):
+        at = jnp.where(i < 3, i, i + 14)
+        zero.coefficients(at, 0, 20, z_mask(at, 0, 2))
+
+    loop(6, outer_coefficients, 2)
+
+    def side_coefficients(i):
+        for low in (0, 17):
+            zero.coefficients(3 + i, low, 3, None)
+
+    loop(14, side_coefficients, 7)
+
+    def outer_smooth(i):
+        zero.smooth(jnp.where(i < 3, i + 1, i + 13), 1, 18)
+
+    loop(6, outer_smooth, 2)
+
+    def side_smooth(i):
+        for low in (1, 16):
+            zero.smooth(4 + i, low, 3)
+
+    loop(12, side_smooth, 6)
 
     for at in (0, 19):
         zero.smo[at] = zero.val[at]
@@ -729,20 +739,24 @@
 
     loop(18, correct_zero, 3)
 
-    def finish_zero(i):
-        for low in (2, 10):
-            staged[i, pl.ds(low - 2, 8)] = zero.finish(i + 2, low, 8)
-
-    loop(16, finish_zero, 4)
-
     stores = []
-    for group, dst in enumerate((out_a, out_b)):
-        for part in range(4):
-            copy = pltpu.make_async_copy(
-                staged.at[:, :, 4 * group + part], dst.at[:, :, pl.ds(128 * part, 128)], out_sem.at[4 * group + part]
-            )
-            copy.start()
-            stores.append(copy)
+    for begin, count in ((0, 8), (8, 4), (12, 4)):
+
+        def finish_zero(i, begin=begin):
+            for low in (2, 10):
+                staged[begin + i, pl.ds(low - 2, 8)] = zero.finish(begin + i + 2, low, 8)
+
+        loop(count, finish_zero, 4)
+        planes = pl.ds(begin, count)
+        for group, dst in enumerate((out_a, out_b)):
+            for part in range(4):
+                copy = pltpu.make_async_copy(
+                    staged.at[planes, :, 4 * group + part],
+                    dst.at[planes, :, pl.ds(128 * part, 128)],
+                    out_sem.at[len(stores)],
+                )
+                copy.start()
+                stores.append(copy)
     for copy in sent:
         copy.wait_send()
     for slot, ref in ((0, whole[0].mob), (1, whole[0].src)):
@@ -775,7 +789,7 @@
     shapes.append(pltpu.VMEM((2, 8, 128), F32))
     shapes.append(pltpu.VMEM((2, 8, 128), F32))
     dma = pltpu.SemaphoreType.DMA
-    shapes += [dma((12,)), dma((8,)), dma((7, 8)), dma((7, 8)), dma((2, 3)), dma((2, 2)), pltpu.SemaphoreType.REGULAR((3,))]
+    shapes += [dma((12,)), dma((24,)), dma((7, 8)), dma((7, 8)), dma((2, 3)), dma((2, 2)), pltpu.SemaphoreType.REGULAR((3,))]
     return shapes
 
 

time: 64 us -> 66.4 us (1.038)
  Pallas kernels: 60.5 us -> 62.9 us
    pallas_call x1, Pallas kernels: 60.5 us -> 62.9 us  [per_device(): pl.pallas_call(kernel, out_shape=(shape, shape), in_specs=[pl.BlockSpec(m...]
where the time goes in v2:
time: 66.4 us; the launch traced here: 66.3 us
  Pallas kernels  62.9 us (95%)
  local copies, waits for them, and re-layouts  2.74 us (4%)
    pallas_call x1, Pallas kernels, per_device(): pl.pallas_call(kernel, out_shape=(shape, shape), in_specs=[pl.BlockSpec(m...  62.9 us
    unnamed x4, local copies, waits for them, and re-layouts  2.74 us

profile of v2, /device:TPU:1, one launch (start us, length us, event | category | flops | bytes accessed | tf_op | source)
XLA Modules:
  0.0 66.3 jit_solution(14530473064594926447)
XLA Ops:
  0.6 62.9 %shard_map.50 = (f32[16,16,512]{2,1,0:T(8,128)}, f32[16,16,512]{2,1,0:T(8,128)}) custom-call(f32[16,16,512]{2,1,0:T(8,128)} %rhs.1, f32[16,16,512]{2,1,0:T(8,128)} %cot.1, s32[16,16,512]{2,1,0:T(8,128)} %phase.1), custom_call_target="tpu_custom_call" | custom-call | tf_op jit(solution)/shard_map/pallas_call | solution.py:798
  63.5 0.0 copy-start
  63.5 1.9 %copy.7 = f32[16,16,512]{2,1,0:T(8,128)} copy(f32[16,16,512]{2,1,0:T(8,128)} %get-tuple-element.4) | data formatting | bytes 1048576
  65.5 0.0 copy-done
  65.5 0.8 %copy.8 = f32[16,16,512]{2,1,0:T(8,128)} copy(f32[16,16,512]{2,1,0:T(8,128)S(1)} %copy-done) | data formatting | bytes 1048576
Async XLA Ops:
  63.5 2.0 %copy-start = (f32[16,16,512]{2,1,0:T(8,128)S(1)}, f32[16,16,512]{2,1,0:T(8,128)}, u32[]{:S(2)}) copy-start(f32[16,16,512]{2,1,0:T(8,128)} %get-tuple-element.5) | copy-start | bytes 1572868

commit v3 on v2

--- a/solution.py
+++ b/solution.py
@@ -18,9 +18,9 @@
 C2 = 2.0 * SECOND / HALF
 LIGHT = 1.0
 HEAVY = 1.0 / 8.0
-AROUND = ((1, 1), (1, -1), (-1, 1), (-1, -1), (1, 0), (-1, 0), (0, 1), (0, -1))
-FAR_Z = (8, 7, 9, 6, 10, 5, 11, 4, 12, 3, 13, 2, 14, 1, 15)
-FAR_Y = (10, 6, 9, 11, 14, 7, 5, 13, 2, 8, 15, 1, 3, 12, 4)
+AROUND = ((1, 0), (-1, 0), (1, 1), (1, -1), (-1, 1), (-1, -1), (0, 1), (0, -1))
+FAR_Z = tuple(range(1, 16))
+FAR_Y = tuple(range(1, 16))
 F32 = jnp.float32
 
 
@@ -288,7 +288,7 @@
     lax.fori_loop(0, count, step, 0, unroll=unroll)
 
 
-def kernel(rhs, cot, phase, out_a, out_b, *scratch):
+def kernel(rhs, cot, phase, both, *scratch):
     scratch = list(scratch)
 
     def take(count):
@@ -312,6 +312,10 @@
 
     def to(dy, dz):
         return {"gy": lax.rem(gy + dy + RING, RING), "gz": lax.rem(gz + dz + RING, RING)}
+
+    barrier = pltpu.get_barrier_semaphore()
+    for dy, dz in AROUND:
+        pl.semaphore_signal(barrier, inc=1, device_id=to(dy, dz), device_id_type=MESH)
 
     loads = []
     for group, (src, dst, first) in enumerate(((phase, phases, 0), (rhs, zero.src, 0), (cot, zero.src, 4))):
@@ -327,9 +331,6 @@
             parts.append(copy)
         loads.append(parts)
 
-    barrier = pltpu.get_barrier_semaphore()
-    for dy, dz in AROUND:
-        pl.semaphore_signal(barrier, inc=1, device_id=to(dy, dz), device_id_type=MESH)
 
     for level in whole:
         count = level.val.shape[0]
@@ -350,7 +351,7 @@
         found = jnp.where(values == 1, HEAVY, LIGHT).astype(F32) * mask
         return sub_take(found, lambda s: s % 4)
 
-    for copy in loads[0] + loads[1] + loads[2]:
+    for copy in loads[0]:
         copy.wait()
     pl.semaphore_wait(barrier, len(AROUND))
 
@@ -368,11 +369,12 @@
             return low + size - width, low - width, width
         return low, low + size, width
 
-    def exchange(slot, ref, z_geometry, y_geometry, rows=None):
+    def exchange(slot, ref, z_geometry, y_geometry, rows=None, corner=None):
         copies = []
         for number, (dy, dz) in enumerate(AROUND):
-            z_from, z_to, z_count = edges(dz, *z_geometry)
-            y_from, y_to, y_count = edges(dy, *y_geometry)
+            both = corner is not None and dy != 0 and dz != 0
+            z_from, z_to, z_count = edges(dz, *(z_geometry[:2] + (corner,) if both else z_geometry))
+            y_from, y_to, y_count = edges(dy, *(y_geometry[:2] + (corner,) if both else y_geometry))
             src = (pl.ds(z_from, z_count), pl.ds(y_from, y_count))
             dst = (pl.ds(z_to, z_count), pl.ds(y_to, y_count))
             if rows is not None:
@@ -435,8 +437,10 @@
         pltpu.make_async_copy(part, part, semaphore).wait()
 
     sent = []
-    phase_halo = exchange(0, phases, (3, 16, 3), (3, 16, 3), 4)
-    source_halo = exchange(1, zero.src, (2, 16, 2), (2, 16, 2))
+    phase_halo = exchange(0, phases, (3, 16, 3), (3, 16, 3), 4, 2)
+    for copy in loads[1] + loads[2]:
+        copy.wait()
+    source_halo = exchange(1, zero.src, (2, 16, 2), (2, 16, 2), None, 1)
     def own_mobility(i):
         total = None
         for plane in (0, 1):
@@ -528,11 +532,10 @@
             total = zero.remainder(2 + 2 * i, low, 8) + zero.remainder(3 + 2 * i, low, 8)
             one.src[4 + i, pl.ds(2 + 2 * half, 2)] = restrict_0(total)
 
-    loop(8, remainder_zero, 2)
+    loop(8, remainder_zero, 4)
     source_one = exchange(4, one.src, (4, 8, 3), (2, 4, 2))
     sent += source_one
 
-    gather_y(0, whole[0].mob, own_m)
     landed(mob_one)
     landed(mob_two)
 
@@ -586,6 +589,7 @@
     loop(4, remainder_one, 4)
     source_two = exchange(6, two.src, (4, 4, 4), (1, 1, 1))
     sent += source_two
+    gather_y(0, whole[0].mob, own_m)
 
     landed(inverse_two)
     for at in (0, 1, 2, 3, 8, 9, 10, 11):
@@ -600,6 +604,8 @@
     rows_s[...] = restrict_2(pair_sum(two.remainder(4, 4)[:, 1]))
     own_s = gather_z(1, rows_s, whole[0].src)
 
+    gather_y(1, whole[0].src, own_s)
+
     drain(whole[0].mob, far_recv.at[0, 1])
 
     block = (4, 8, 8, 4)
@@ -623,7 +629,6 @@
 
         loop(steps[number], coefficients, steps[number])
 
-    gather_y(1, whole[0].src, own_s)
     drain(whole[0].src, far_recv.at[1, 1])
 
     for number, level in enumerate(whole[:-1]):
@@ -731,7 +736,7 @@
         for plane in (0, 1):
             zero.val[2 * i + plane] = zero.smo[2 * i + plane] + added
 
-    loop(10, add_zero, 2)
+    loop(10, add_zero, 5)
 
     def correct_zero(i):
         for low in (1, 10):
@@ -748,7 +753,7 @@
 
         loop(count, finish_zero, 4)
         planes = pl.ds(begin, count)
-        for group, dst in enumerate((out_a, out_b)):
+        for group, dst in enumerate((both.at[0], both.at[1])):
             for part in range(4):
                 copy = pltpu.make_async_copy(
                     staged.at[planes, :, 4 * group + part],
@@ -794,17 +799,18 @@
 
 
 def per_device(right_side, cotangent, phase):
-    shape = jax.ShapeDtypeStruct(right_side.shape, F32)
-    return pl.pallas_call(
+    shape = jax.ShapeDtypeStruct((2,) + right_side.shape, F32)
+    both = pl.pallas_call(
         kernel,
-        out_shape=(shape, shape),
+        out_shape=shape,
         in_specs=[pl.BlockSpec(memory_space=pl.ANY)] * 3,
-        out_specs=(pl.BlockSpec(memory_space=pl.ANY),) * 2,
+        out_specs=pl.BlockSpec(memory_space=pl.ANY),
         scratch_shapes=scratch_shapes(),
         compiler_params=pltpu.CompilerParams(
             collective_id=0, has_side_effects=True, vmem_limit_bytes=62 * 2**20
         ),
     )(right_side, cotangent, phase)
+    return both[0], both[1]
 
 
 def solution(mesh):

time: 66.4 us -> 61.7 us (0.929)
  Pallas kernels: 62.9 us -> 58.1 us
    pallas_call x1, Pallas kernels: 62.9 us -> 58.1 us  [per_device(): pl.pallas_call(kernel, out_shape=shape, in_specs=[pl.BlockSpec(memory_spa...]
    unnamed x4 -> x0, local copies, waits for them, and re-layouts: 2.74 us -> none
    squeeze x0 -> x1, local copies, waits for them, and re-layouts: none -> 2.28 us  [per_device(): return (both[0], both[1])]
where the time goes in v3:
time: 61.7 us; the launch traced here: 61 us
  Pallas kernels  58.1 us (94%)
  local copies, waits for them, and re-layouts  2.28 us (4%)
  between operations  0.64 us (1%)
    pallas_call x1, Pallas kernels, per_device(): pl.pallas_call(kernel, out_shape=shape, in_specs=[pl.BlockSpec(memory_spa...  58.1 us
    squeeze x1, local copies, waits for them, and re-layouts, per_device(): return (both[0], both[1])  2.28 us

profile of v3, /device:TPU:1, one launch (start us, length us, event | category | flops | bytes accessed | tf_op | source)
XLA Modules:
  0.0 61.0 jit_solution(13587344178721659626)
XLA Ops:
  0.6 58.1 %shard_map.50 = f32[2,16,16,512]{3,2,1,0:T(8,128)} custom-call(f32[16,16,512]{2,1,0:T(8,128)} %rhs.1, f32[16,16,512]{2,1,0:T(8,128)} %cot.1, s32[16,16,512]{2,1,0:T(8,128)} %phase.1), custom_call_target="tpu_custom_call" | custom-call | tf_op jit(solution)/shard_map/pallas_call | solution.py:803
  58.7 2.3 %slice_bitcast_fusion = (f32[16,16,512]{2,1,0:T(8,128)}, f32[16,16,512]{2,1,0:T(8,128)}) fusion(f32[2,16,16,512]{3,2,1,0:T(8,128)} %shard_map.50), kind=kLoop, calls=%fused_computation | loop fusion | bytes 2097152 | tf_op jit(solution)/shard_map/squeeze | solution.py:813

commit v4 on v3

--- a/solution.py
+++ b/solution.py
@@ -589,7 +589,6 @@
     loop(4, remainder_one, 4)
     source_two = exchange(6, two.src, (4, 4, 4), (1, 1, 1))
     sent += source_two
-    gather_y(0, whole[0].mob, own_m)
 
     landed(inverse_two)
     for at in (0, 1, 2, 3, 8, 9, 10, 11):
@@ -603,6 +602,7 @@
         two.smo[at] = two.val[at]
     rows_s[...] = restrict_2(pair_sum(two.remainder(4, 4)[:, 1]))
     own_s = gather_z(1, rows_s, whole[0].src)
+    gather_y(0, whole[0].mob, own_m)
 
     gather_y(1, whole[0].src, own_s)
 

time: 61.7 us -> 60.6 us (0.982); the launches traced: 61 us -> 60.5 us
  no operation moved by 1% of the time
where the time goes in v4:
time: 60.6 us; the launch traced here: 60.5 us
  Pallas kernels  57.6 us (95%)
  local copies, waits for them, and re-layouts  2.28 us (4%)
  between operations  0.64 us (1%)
    pallas_call x1, Pallas kernels, per_device(): pl.pallas_call(kernel, out_shape=shape, in_specs=[pl.BlockSpec(memory_spa...  57.6 us
    squeeze x1, local copies, waits for them, and re-layouts, per_device(): return (both[0], both[1])  2.28 us

profile of v4, /device:TPU:1, one launch (start us, length us, event | category | flops | bytes accessed | tf_op | source)
XLA Modules:
  0.0 60.5 jit_solution(18189631200802364567)
XLA Ops:
  0.6 57.6 %shard_map.50 = f32[2,16,16,512]{3,2,1,0:T(8,128)} custom-call(f32[16,16,512]{2,1,0:T(8,128)} %rhs.1, f32[16,16,512]{2,1,0:T(8,128)} %cot.1, s32[16,16,512]{2,1,0:T(8,128)} %phase.1), custom_call_target="tpu_custom_call" | custom-call | tf_op jit(solution)/shard_map/pallas_call | solution.py:803
  58.2 2.3 %slice_bitcast_fusion = (f32[16,16,512]{2,1,0:T(8,128)}, f32[16,16,512]{2,1,0:T(8,128)}) fusion(f32[2,16,16,512]{3,2,1,0:T(8,128)} %shard_map.50), kind=kLoop, calls=%fused_computation | loop fusion | bytes 2097152 | tf_op jit(solution)/shard_map/squeeze | solution.py:813

commit v5 on v4

--- a/solution.py
+++ b/solution.py
@@ -300,7 +300,7 @@
     one, two = Level(1, take(11)), Level(2, take(11))
     whole = [Level(depth, take(11)) for depth in range(3, 7)]
     answers = take(5)
-    phases, staged, rows_m, rows_s = take(4)
+    phases, staged, rows_m, rows_s, packed_m = take(5)
     in_sem, out_sem, near_send, near_recv, far_send, far_recv, known = take(7)
     gy, gz = lax.axis_index("gy"), lax.axis_index("gz")
 
@@ -395,17 +395,19 @@
         for copy in copies:
             copy.wait_recv()
 
-    def place(ref):
-        return ref.at[pl.ds(2 * gz + 1, 2), gy // 4, pl.ds(2 * lax.rem(gy, 4), 2)]
+    def place(slot, ref):
+        planes = pl.ds(gz, 1) if slot == 0 else pl.ds(2 * gz + 1, 2)
+        return ref.at[planes, gy // 4, pl.ds(2 * lax.rem(gy, 4), 2)]
 
     def gather_z(slot, rows, ref):
-        own = pltpu.make_async_copy(rows.at[pl.ds(0, 2), pl.ds(0, 2)], place(ref), far_send.at[slot, 2])
+        part = rows.at[pl.ds(0, 1 + slot), pl.ds(0, 2)]
+        own = pltpu.make_async_copy(part, place(slot, ref), far_send.at[slot, 2])
         own.start()
 
         for away in FAR_Z:
             pltpu.make_async_remote_copy(
-                src_ref=rows.at[pl.ds(0, 2), pl.ds(0, 2)],
-                dst_ref=place(ref),
+                src_ref=part,
+                dst_ref=place(slot, ref),
                 send_sem=far_send.at[slot, 0],
                 recv_sem=far_recv.at[slot, 0],
                 device_id=to_z(away),
@@ -414,13 +416,14 @@
         return own
 
     def settle(ref, semaphore, planes):
-        part = ref.at[pl.ds(1, planes), 0, pl.ds(0, 2)]
+        part = ref.at[pl.ds(0, planes), 0, pl.ds(0, 2)]
         pltpu.make_async_copy(part, part, semaphore).wait()
 
     def gather_y(slot, ref, own):
         own.wait()
-        settle(ref, far_recv.at[slot, 0], 2 * (RING - 1))
-        part = ref.at[pl.ds(1, 32), gy // 4, pl.ds(2 * lax.rem(gy, 4), 2)]
+        settle(ref, far_recv.at[slot, 0], (1 + slot) * (RING - 1))
+        planes = pl.ds(0, 16) if slot == 0 else pl.ds(1, 32)
+        part = ref.at[planes, gy // 4, pl.ds(2 * lax.rem(gy, 4), 2)]
 
         for away in FAR_Y:
             pltpu.make_async_remote_copy(
@@ -432,8 +435,8 @@
                 device_id_type=MESH,
             ).start()
 
-    def drain(ref, semaphore):
-        part = ref.at[pl.ds(1, 30)]
+    def drain(slot, ref, semaphore):
+        part = ref.at[pl.ds(0, 15 + 15 * slot)]
         pltpu.make_async_copy(part, part, semaphore).wait()
 
     sent = []
@@ -452,7 +455,8 @@
 
     loop(8, own_mobility, 2)
     two.mob[pl.ds(4, 4), 1] = restrict_1(pair_sum(one.mob[pl.ds(4, 8), pl.ds(2, 4)]))
-    rows_m[...] = restrict_2(pair_sum(two.mob[pl.ds(4, 4), 1]))
+    found = restrict_2(pair_sum(two.mob[pl.ds(4, 4), 1]))
+    rows_m[0] = jnp.where(lane_iota((8, 128)) < 64, found[0], found[1])
     mob_one = exchange(2, one.mob, (4, 8, 4), (2, 4, 2))
     mob_two = exchange(3, two.mob, (4, 4, 4), (1, 1, 1))
     sent += phase_halo + source_halo + mob_one + mob_two
@@ -476,7 +480,7 @@
 
     loop(12, inner_smooth, 3)
     pl.semaphore_wait(known.at[2], 4)
-    own_m = gather_z(0, rows_m, whole[0].mob)
+    own_m = gather_z(0, rows_m, packed_m)
     landed(phase_halo)
 
     def outer_mobility(i):
@@ -602,11 +606,20 @@
         two.smo[at] = two.val[at]
     rows_s[...] = restrict_2(pair_sum(two.remainder(4, 4)[:, 1]))
     own_s = gather_z(1, rows_s, whole[0].src)
-    gather_y(0, whole[0].mob, own_m)
+    gather_y(0, packed_m, own_m)
 
     gather_y(1, whole[0].src, own_s)
 
-    drain(whole[0].mob, far_recv.at[0, 1])
+    drain(0, packed_m, far_recv.at[0, 1])
+
+    def unpack(i):
+        found = packed_m[pl.ds(2 * i, 2)]
+        turned = lane_roll(found, 64)
+        low = lane_iota(found.shape) < 64
+        pair = jnp.stack([jnp.where(low, found, turned), jnp.where(low, turned, found)], axis=1)
+        whole[0].mob[pl.ds(1 + 4 * i, 4)] = pair.reshape((4, 4, 8, 128))
+
+    loop(8, unpack, 4)
 
     block = (4, 8, 8, 4)
     steps = (8, 2, 1, 1)
@@ -629,7 +642,7 @@
 
         loop(steps[number], coefficients, steps[number])
 
-    drain(whole[0].src, far_recv.at[1, 1])
+    drain(1, whole[0].src, far_recv.at[1, 1])
 
     for number, level in enumerate(whole[:-1]):
         size = block[number]
@@ -764,9 +777,9 @@
                 stores.append(copy)
     for copy in sent:
         copy.wait_send()
-    for slot, ref in ((0, whole[0].mob), (1, whole[0].src)):
-        settle(ref, far_send.at[slot, 0], 2 * (RING - 1))
-        drain(ref, far_send.at[slot, 1])
+    for slot, ref in ((0, packed_m), (1, whole[0].src)):
+        settle(ref, far_send.at[slot, 0], (1 + slot) * (RING - 1))
+        drain(slot, ref, far_send.at[slot, 1])
     for copy in stores:
         copy.wait()
 
@@ -793,6 +806,7 @@
     arrays(16, 16, 1)
     shapes.append(pltpu.VMEM((2, 8, 128), F32))
     shapes.append(pltpu.VMEM((2, 8, 128), F32))
+    arrays(16, 4, 1)
     dma = pltpu.SemaphoreType.DMA
     shapes += [dma((12,)), dma((24,)), dma((7, 8)), dma((7, 8)), dma((2, 3)), dma((2, 2)), pltpu.SemaphoreType.REGULAR((3,))]
     return shapes

time: 60.6 us -> 60.2 us (level)
  no operation moved by 1% of the time
where the time goes in v5:
time: 60.2 us; the launch traced here: 60.1 us
  Pallas kernels  57.2 us (95%)
  local copies, waits for them, and re-layouts  2.28 us (4%)
  between operations  0.64 us (1%)
    pallas_call x1, Pallas kernels, per_device(): pl.pallas_call(kernel, out_shape=shape, in_specs=[pl.BlockSpec(memory_spa...  57.2 us
    squeeze x1, local copies, waits for them, and re-layouts, per_device(): return (both[0], both[1])  2.28 us

profile of v5, /device:TPU:1, one launch (start us, length us, event | category | flops | bytes accessed | tf_op | source)
XLA Modules:
  0.0 60.1 jit_solution(12804559228692963292)
XLA Ops:
  0.6 57.2 %shard_map.50 = f32[2,16,16,512]{3,2,1,0:T(8,128)} custom-call(f32[16,16,512]{2,1,0:T(8,128)} %rhs.1, f32[16,16,512]{2,1,0:T(8,128)} %cot.1, s32[16,16,512]{2,1,0:T(8,128)} %phase.1), custom_call_target="tpu_custom_call" | custom-call | tf_op jit(solution)/shard_map/pallas_call | solution.py:817
  57.8 2.3 %slice_bitcast_fusion = (f32[16,16,512]{2,1,0:T(8,128)}, f32[16,16,512]{2,1,0:T(8,128)}) fusion(f32[2,16,16,512]{3,2,1,0:T(8,128)} %shard_map.50), kind=kLoop, calls=%fused_computation | loop fusion | bytes 2097152 | tf_op jit(solution)/shard_map/squeeze | solution.py:827
